TPU v7x, 32 devices: a whole 2x2x4 slice. The times are simulated.
32 devices in a mesh: ga: 4 (over z), ka: 8 (over y, x, core).
Axes of the slice: x: 2, y: 2, z: 4, core: 2. Of those that a mesh axis runs over, the one named last changes fastest.
Arguments:
- amplitudes: float32 [14400, 2048], P(None, ('ka', 'ga')), may hold values from -6 to 6
- integrals: float32 [2048, 15360], P('ga', 'ka'), may hold values from -0.125 to 0.125
Outputs:
- residual: float32 [14400, 15360], P('ga', 'ka')
All inputs are finite; a program needn't handle non-finite values.
Results may differ from a plain program's by a relative error of at most 0.00007.
Values sent between devices are 32-bit elements; how exact they have to be, the bound alone decides.
No kernel may reach another device: no remote copies, remote signals or barrier semaphores. Data moves between devices by JAX's collectives and lax.ppermute only.
A program may use at most 128 MiB of HBM per device.

v0:
```python
import jax
import jax.numpy as jnp
from jax import lax
from jax.sharding import PartitionSpec as P


def per_device(amplitudes, integrals):
    regrouped = lax.all_to_all(amplitudes, "ga", split_axis=0, concat_axis=1, tiled=True)
    full_rows = lax.all_gather(regrouped, "ka", axis=1, tiled=True)
    ladder = jnp.dot(
        full_rows,
        lax.all_gather(integrals, "ga", axis=0, tiled=True),
        precision=lax.Precision.HIGHEST,
        preferred_element_type=jnp.float32,
    )
    return 0.5 * ladder


def solution(mesh):
    placed = (P(None, ("ka", "ga")), P("ga", "ka"))
    return jax.shard_map(
        per_device, mesh=mesh, in_specs=placed, out_specs=P("ga", "ka"), check_vma=False
    )
```

profile of v0, /device:TPU:16, one launch (start us, length us, event | category | flops | bytes accessed | tf_op | source)
XLA Modules:
  0.0 718.2 jit_solution(5958930319926723546)
XLA Ops:
  6.5 0.0 all-gather.5.cloned.1.call-start
  6.5 0.7 all-gather.5.cloned.1.call-update
  7.3 0.0 all-gather.3.cloned.1.call-start
  7.3 5.7 all_to_all.14
  13.0 2.3 copy.3
  15.4 190.2 %all_to_all.19 = f32[4,3600,64]{1,2,0:T(8,128)} all-to-all(f32[4,3600,64]{1,2,0:T(8,128)S(1)} %copy.3), channel_id=1, replica_groups=mesh['ga'=4,'ka'=8] {'ga'}, dimensions={0} | all-to-all | bytes 7372800 | tf_op jit(solution)/shard_map/all_to_all | solution.py:8
  205.5 0.0 all-gather.3.cloned.1.call-update
  205.6 149.2 %all-gather.5.cloned.1.call-done = f32[2048,1920]{1,0:T(8,128)} async-done(((f32[512,1920]{1,0:T(8,128)}), f32[2048,1920]{1,0:T(8,128)}) %all-gather.5.cloned.1.call-update) | async-done | bytes 15728656 | tf_op jit(solution)/shard_map/all_gather | solution.py:12
  354.8 151.7 %all-gather.3.cloned.1.call-done = f32[3600,2048]{0,1:T(8,128)} async-done(((f32[3600,256]{0,1:T(8,128)}), f32[3600,2048]{0,1:T(8,128)}) %all-gather.3.cloned.1.call-update) | async-done | bytes 29491216 | tf_op jit(solution)/shard_map/all_gather | solution.py:9
  506.4 204.9 %convolution_multiply_fusion = f32[3600,1920]{1,0:T(8,128)} fusion(f32[3600,2048]{0,1:T(8,128)} %all-gather.3.cloned.1.call-done, f32[2048,1920]{1,0:T(8,128)} %all-gather.5.cloned.1.call-done), kind=kOutput, calls=%fused_computation | convolution fusion | flops 169876226048 | bytes 72867840 | tf_op jit(solution)/shard_map/dot_general | solution.py:10
Async XLA Ops:
  6.5 348.2 %all-gather.5.cloned.1.call-start = ((), (), s32[]{:S(2)}) async-start(), calls=%async_computation.2 | async-start | bytes 19660800 | tf_op jit(solution)/shard_map/all_gather | solution.py:12
  7.3 499.2 %all-gather.3.cloned.1.call-start = ((), (), s32[]{:S(2)}) async-start(), calls=%async_computation.1 | async-start | bytes 34209792 | tf_op jit(solution)/shard_map/all_gather | solution.py:9
Sparse Core Ops, SparseCore 0:
  8.9 345.7 all-gather.4
  356.6 149.7 all-gather.2
where the time goes:
time: 720 us; the launch traced here: 718 us
  waiting for transfers between devices  302 us (42%)
  matrix products  205 us (28%)
  blocking collectives  190 us (26%)
  between operations  13.4 us (2%)
  local copies, waits for them, and re-layouts  8.06 us (1%)
    dot_general x1, matrix products, per_device(): jnp.dot(full_rows, lax.all_gather(integrals, 'ga', axis=0, tiled=True), p...  205 us
    all_to_all x1, blocking collectives, per_device(): lax.all_to_all(amplitudes, 'ga', split_axis=0, concat_axis=1, tiled=True)  190 us
    all_gather x1, waiting for transfers between devices, per_device(): full_rows = lax.all_gather(regrouped, 'ka', axis=1, tiled=True)  152 us
    all_gather x1, waiting for transfers between devices, per_device(): lax.all_gather(integrals, 'ga', axis=0, tiled=True)  149 us
  transfers between devices with their start and end apart: 2, of which 2 were waited for; matrix products, arithmetic and copies ran while one was open for 0% of the time, Pallas kernels for 0%

commit v1 on v0

v1 whole, which is shorter than its diff:
```python
import functools

import jax
import jax.numpy as jnp
from jax import lax
from jax.experimental import pallas as pl
from jax.experimental.pallas import tpu as pltpu
from jax.sharding import PartitionSpec as P

ROWS = 240
WIDE = 512


def chunks_of(columns):
    wide = [(start, WIDE, WIDE) for start in range(0, columns - WIDE + 1, WIDE)]
    start = len(wide) * WIDE
    left = columns - start
    if left == 384:
        return [(start, 256, 256), *wide, (start + 256, 128, 128)]
    return wide + ([(start, left, WIDE)] if left else [])


def turn_kernel(t_ref, first_ref, second_ref):
    turned = t_ref[...].T
    half = turned.shape[1] // 2
    first_ref[...] = turned[:, :half]
    second_ref[...] = turned[:, half:]


def turn(columns):
    depth, rows = columns.shape
    width = 512
    half = jax.ShapeDtypeStruct((rows, depth // 2), jnp.float32)
    return pl.pallas_call(
        turn_kernel,
        grid=(pl.cdiv(rows, width),),
        in_specs=[pl.BlockSpec((depth, width), lambda i: (0, i))],
        out_specs=[pl.BlockSpec((width, depth // 2), lambda i: (i, 0))] * 2,
        out_shape=[half, half],
        cost_estimate=pl.CostEstimate(
            flops=0, bytes_accessed=8 * depth * rows, transcendentals=0
        ),
    )(columns)


def split(x):
    high = x.astype(jnp.bfloat16)
    return high, (x - high.astype(jnp.float32)).astype(jnp.bfloat16)


def product_kernel(blocks, place_ref, *refs):
    parts = refs[:blocks]
    w_ref = refs[blocks]
    out_ref, t_high, t_low, w_high, w_low = refs[-5:]
    half = parts[0].shape[1]

    @pl.when(pl.program_id(0) == 0)
    def _():
        for n in range(blocks // 2):
            start = pl.multiple_of((place_ref[0] ^ n) * 2 * half, 2 * half)
            high, low = split(w_ref[pl.ds(start, 2 * half), :])
            w_high[pl.ds(n * 2 * half, 2 * half), :] = high
            w_low[pl.ds(n * 2 * half, 2 * half), :] = low

    for n in range(blocks):
        high, low = split(parts[n][...])
        t_high[:, n * half : (n + 1) * half] = high
        t_low[:, n * half : (n + 1) * half] = low
    dot = functools.partial(jnp.dot, preferred_element_type=jnp.float32)
    total = dot(t_low[...], w_high[...])
    total += dot(t_high[...], w_low[...])
    total += dot(t_high[...], w_high[...])
    out_ref[:, : w_ref.shape[1]] = 0.5 * total


def product(place, parts, w, out, start, block, full):
    blocks = len(parts)
    rows, half = parts[0].shape
    depth, width = w.shape
    operands = [place, *parts, w]
    in_specs = [pl.BlockSpec((ROWS, half), lambda i, p: (i, 0))] * blocks
    in_specs.append(pl.BlockSpec((depth, width), lambda i, p: (0, 0)))
    aliases = {}
    if out is not None:
        aliases = {len(operands): 0}
        operands.append(out)
        in_specs.append(pl.BlockSpec(memory_space=pl.ANY))
    return pl.pallas_call(
        functools.partial(product_kernel, blocks),
        grid_spec=pltpu.PrefetchScalarGridSpec(
            num_scalar_prefetch=1,
            grid=(pl.cdiv(rows, ROWS),),
            in_specs=in_specs,
            out_specs=pl.BlockSpec((ROWS, block), lambda i, p: (i, start // block)),
            scratch_shapes=[
                pltpu.VMEM((ROWS, depth), jnp.bfloat16),
                pltpu.VMEM((ROWS, depth), jnp.bfloat16),
                pltpu.VMEM((depth, width), jnp.bfloat16),
                pltpu.VMEM((depth, width), jnp.bfloat16),
            ],
        ),
        out_shape=jax.ShapeDtypeStruct((rows, full), jnp.float32),
        input_output_aliases=aliases,
        compiler_params=pltpu.CompilerParams(vmem_limit_bytes=40 * 2**20),
        cost_estimate=pl.CostEstimate(
            flops=6 * rows * depth * width,
            bytes_accessed=4 * (rows * depth + depth * width + rows * width),
            transcendentals=0,
        ),
    )(*operands)


def per_device(devices, amplitudes, integrals):
    swap = lambda x, mask: lax.ppermute(x, "ka", [(d, d ^ mask) for d in range(devices)])
    regrouped = lax.all_to_all(amplitudes, "ga", split_axis=0, concat_axis=1, tiled=True)
    chunks = chunks_of(integrals.shape[1])

    def gather(chunk, source):
        piece = lax.slice_in_dim(source, chunk[0], chunk[0] + chunk[1], axis=1)
        return lax.all_gather(piece, "ga", axis=0, tiled=True)

    pieces = [gather(chunks[0], integrals)]
    regrouped, later = lax.optimization_barrier((regrouped, integrals))
    pieces += [gather(chunk, later) for chunk in chunks[1:]]

    masks = [1 << bit for bit in range(1, devices.bit_length() - 1)]
    halves = []
    for half, order in zip(turn(regrouped.T), (masks[::-1], masks)):
        held = {0: half}
        for mask in (*order, 1):
            held |= {n ^ mask: swap(block, mask) for n, block in held.items()}
        halves.append(held)
    parts = [held[n] for n in range(devices) for held in halves]

    place = lax.axis_index("ka").astype(jnp.int32).reshape(1)
    out = None
    for (start, _, block), piece in zip(chunks, pieces):
        out = product(place, parts, piece, out, start, block, integrals.shape[1])
    return out


def solution(mesh):
    placed = (P(None, ("ka", "ga")), P("ga", "ka"))
    return jax.shard_map(
        functools.partial(per_device, mesh.shape["ka"]),
        mesh=mesh,
        in_specs=placed,
        out_specs=P("ga", "ka"),
        check_vma=False,
    )
```

time: 720 us -> 469 us (0.65)
  matrix products: 205 us -> 0 us
  blocking collectives: 190 us -> 0 us
  Pallas kernels: 0 us -> 142 us
  waiting for transfers between devices: 302 us -> 231 us
  local copies, waits for them, and re-layouts: 8.06 us -> 64.3 us
  starting transfers between devices: 0.04 us -> 12.6 us
    all_gather x2 -> x5, waiting for transfers between devices: 301 us -> 0.07 us  [gather(): return lax.all_gather(piece, 'ga', axis=0, tiled=True)]
    dot_general x1 -> x0, matrix products: 205 us -> none  [per_device(): jnp.dot(full_rows, lax.all_gather(integrals, 'ga', axis=0, tiled=True), p...]
    all_to_all x1 -> x0, blocking collectives: 190 us -> none  [per_device(): lax.all_to_all(amplitudes, 'ga', split_axis=0, concat_axis=1, tiled=True)]
    pallas_call x0 -> x6, Pallas kernels: none -> 142 us  [the longest x5 135 us: product(): pl.pallas_call(functools.partial(product_kernel, blocks), grid_spec=pltpu...]
    ppermute x0 -> x14, waiting for transfers between devices: none -> 116 us  [per_device(): lax.ppermute(x, 'ka', [(d, d ^ mask) for d in range(devices)])]
    all_to_all x0 -> x1, waiting for transfers between devices: none -> 113 us  [per_device(): lax.all_to_all(amplitudes, 'ga', split_axis=0, concat_axis=1, tiled=True)]
    unnamed x0 -> x66, local copies, waits for them, and re-layouts: none -> 47.2 us
  transfers between devices with their start and end apart: 2 -> 20, of which waited for: 2 -> 9; matrix products, arithmetic and copies ran while one was open for 0% -> 2% of each run, Pallas kernels for 0% -> 26%
where the time goes in v1:
time: 469 us; the launch traced here: 463 us
  waiting for transfers between devices  231 us (49%)
  Pallas kernels  142 us (30%)
  local copies, waits for them, and re-layouts  64.3 us (14%)
  between operations  13.3 us (3%)
  starting transfers between devices  12.6 us (3%)
    pallas_call x5, Pallas kernels, product(): pl.pallas_call(functools.partial(product_kernel, blocks), grid_spec=pltpu...  135 us
    ppermute x14, waiting for transfers between devices, per_device(): lax.ppermute(x, 'ka', [(d, d ^ mask) for d in range(devices)])  116 us
    all_to_all x1, waiting for transfers between devices, per_device(): lax.all_to_all(amplitudes, 'ga', split_axis=0, concat_axis=1, tiled=True)  113 us
    unnamed x66, local copies, waits for them, and re-layouts  47.2 us
    all_to_all x2, local copies, waits for them, and re-layouts, per_device(): lax.all_to_all(amplitudes, 'ga', split_axis=0, concat_axis=1, tiled=True)  9.9 us
  transfers between devices with their start and end apart: 20, of which 9 were waited for; matrix products, arithmetic and copies ran while one was open for 2% of the time, Pallas kernels for 26%

profile of v1, /device:TPU:16, one launch (start us, length us, event | category | flops | bytes accessed | tf_op | source)
XLA Modules:
  0.0 462.8 jit_solution(6434450586430391948)
XLA Ops:
  6.5 5.7 %all_to_all.14 = f32[4,3600,64]{1,0,2:T(4,128)} reshape(f32[14400,64]{0,1:T(8,128)} %param.2) | data formatting | bytes 7372800 | tf_op jit(solution)/shard_map/all_to_all | solution.py:115
  12.3 4.2 copy.7
  16.4 5.2 %all-to-all-start = ((f32[4,3600,64]{1,2,0:T(8,128)}), f32[4,3600,64]{1,2,0:T(8,128)}, u32[]{:S(2)}, u32[]{:S(2)}) async-start(f32[4,3600,64]{1,2,0:T(8,128)} %copy.7), calls=%async_computation | async-start | bytes 7602176 | tf_op jit(solution)/shard_map/all_to_all | solution.py:115
  21.6 1.9 slice.19
  23.6 113.3 %all-to-all-done = f32[4,3600,64]{1,2,0:T(8,128)} async-done(((f32[4,3600,64]{1,2,0:T(8,128)}), f32[4,3600,64]{1,2,0:T(8,128)}, u32[]{:S(2)}, u32[]{:S(2)}) %all-to-all-start) | async-done | bytes 3686432 | tf_op jit(solution)/shard_map/all_to_all | solution.py:115
  136.9 3.6 fusion
  142.1 7.0 %shard_map.28 = (f32[3600,128]{1,0:T(8,128)}, f32[3600,128]{1,0:T(8,128)}) custom-call(f32[256,3600]{1,0:T(8,128)} %bitcast.3.t_ref), custom_call_target="tpu_custom_call" | custom-call | bytes 7372800 | tf_op jit(solution)/shard_map/pallas_call | solution.py:34
  149.0 1.5 collective-permute-start.6
  153.1 39.4 %collective-permute-done.6.refs_8_ = f32[3600,128]{1,0:T(8,128)} collective-permute-done((f32[3600,128]{1,0:T(8,128)}, f32[3600,128]{1,0:T(8,128)}, u32[]{:S(2)}, u32[]{:S(2)}) %collective-permute-start.6) | collective-permute-done | bytes 1843232 | tf_op jit(solution)/shard_map/ppermute | solution.py:114
  195.4 38.0 %collective-permute-done.2.refs_4_ = f32[3600,128]{1,0:T(8,128)S(1)} collective-permute-done((f32[3600,128]{1,0:T(8,128)}, f32[3600,128]{1,0:T(8,128)S(1)}, u32[]{:S(2)}, u32[]{:S(2)}) %collective-permute-start.2) | collective-permute-done | bytes 1843232 | tf_op jit(solution)/shard_map/ppermute | solution.py:114
  239.5 31.2 %collective-permute-done.10.refs_12_ = f32[3600,128]{1,0:T(8,128)} collective-permute-done((f32[3600,128]{1,0:T(8,128)}, f32[3600,128]{1,0:T(8,128)}, u32[]{:S(2)}, u32[]{:S(2)}) %collective-permute-start.10) | collective-permute-done | bytes 1843232 | tf_op jit(solution)/shard_map/ppermute | solution.py:114
  273.0 1.7 slice.15
  274.9 2.6 collective-permute-done.12.refs_14_
  277.5 2.6 collective-permute-done.13.refs_15_
  289.2 21.3 %shard_map.29.refs_17_ = f32[3600,1920]{1,0:T(8,128)} custom-call(s32[1]{0:T(128)} %bitcast.place_ref, f32[3600,128]{1,0:T(8,128)S(1)} %copy-done, f32[3600,128]{1,0:T(8,128)S(1)} %copy-done.2, f32[3600,128]{1,0:T(8,128)S(1)} %copy-done.20, f32[3600,128]{1,0:T(8,128)S(1)} %copy-done.26, f32[3600,128]{1,0:T(8,128)S(1)} %copy-done.14, ...), custom_call_target="tpu_custom_call" | custom-call | flops 11324620800 | bytes 35274752 | tf_op jit(solution)/shard_map/pallas_call | solution.py:88
  310.5 1.7 copy-done.3
  312.2 1.7 copy-done.9
  313.9 1.7 copy-done.15
  318.5 30.9 %shard_map.30.refs_17_ = f32[3600,1920]{1,0:T(8,128)} custom-call(s32[1]{0:T(128)} %bitcast.place_ref, f32[3600,128]{1,0:T(8,128)S(1)} %copy-done.1, f32[3600,128]{1,0:T(8,128)S(1)} %copy-done.3, f32[3600,128]{1,0:T(8,128)S(1)} %copy-done.21, f32[3600,128]{1,0:T(8,128)S(1)} %copy-done.27, ...), custom_call_target="tpu_custom_call", output_to_operand_aliasing={{}: (18, {})} | custom-call | flops 22649241600 | bytes 41058304 | tf_op jit(solution)/shard_map/pallas_call | solution.py:88
  357.0 30.9 %shard_map.31.refs_17_ = f32[3600,1920]{1,0:T(8,128)} custom-call(s32[1]{0:T(128)} %bitcast.place_ref, f32[3600,128]{1,0:T(8,128)S(1)} %copy-done.1, f32[3600,128]{1,0:T(8,128)S(1)} %copy-done.4, f32[3600,128]{1,0:T(8,128)S(1)} %copy-done.22, f32[3600,128]{1,0:T(8,128)S(1)} %copy-done.28, ...), custom_call_target="tpu_custom_call", output_to_operand_aliasing={{}: (18, {})} | custom-call | flops 22649241600 | bytes 41058304 | tf_op jit(solution)/shard_map/pallas_call | solution.py:88
  390.9 1.6 copy-done.17
  392.5 1.6 copy-done.23
  395.5 30.9 %shard_map.32.refs_17_ = f32[3600,1920]{1,0:T(8,128)} custom-call(s32[1]{0:T(128)} %bitcast.place_ref, f32[3600,128]{1,0:T(8,128)S(1)} %copy-done.1, f32[3600,128]{1,0:T(8,128)S(1)} %copy-done.5, f32[3600,128]{1,0:T(8,128)S(1)} %copy-done.23, f32[3600,128]{1,0:T(8,128)S(1)} %copy-done.29, ...), custom_call_target="tpu_custom_call", output_to_operand_aliasing={{}: (18, {})} | custom-call | flops 22649241600 | bytes 41058304 | tf_op jit(solution)/shard_map/pallas_call | solution.py:88
  435.2 21.2 %shard_map.33 = f32[3600,1920]{1,0:T(8,128)} custom-call(s32[1]{0:T(128)} %bitcast.place_ref, f32[3600,128]{1,0:T(8,128)S(1)} %copy-done.1, f32[3600,128]{1,0:T(8,128)S(1)} %copy-done.6, f32[3600,128]{1,0:T(8,128)S(1)} %copy-done.24, f32[3600,128]{1,0:T(8,128)S(1)} %copy-done.30, f32[3600,128]{1,0:T(8,128)S(1)} %copy-done.18, ...), custom_call_target="tpu_custom_call", output_to_operand_aliasing={{}: (18, {})} | custom-call | flops 5662310400 | bytes 32382976 | tf_op jit(solution)/shard_map/pallas_call | solution.py:88
  (98 shorter events, 48.4 us)
Async XLA Ops:
  16.4 120.5 %all-to-all-start = ((f32[4,3600,64]{1,2,0:T(8,128)}), f32[4,3600,64]{1,2,0:T(8,128)}, u32[]{:S(2)}, u32[]{:S(2)}) async-start(f32[4,3600,64]{1,2,0:T(8,128)} %copy.7), calls=%async_computation | async-start | bytes 7602176 | tf_op jit(solution)/shard_map/all_to_all | solution.py:115
  21.6 253.1 %all-gather.14.cloned.1.call-start = ((), (), s32[]{:S(2)}) async-start(), calls=%async_computation.5 | async-start | bytes 2621440 | tf_op jit(solution)/shard_map/all_gather | solution.py:120
  23.5 287.0 %all-gather.12.cloned.1.call-start = ((), (), s32[]{:S(2)}) async-start(), calls=%async_computation.4 | async-start | bytes 5242880 | tf_op jit(solution)/shard_map/all_gather | solution.py:120
  140.6 208.9 %all-gather.10.cloned.1.call-start = ((), (), s32[]{:S(2)}) async-start(), calls=%async_computation.3 | async-start | bytes 5242880 | tf_op jit(solution)/shard_map/all_gather | solution.py:120
  141.3 246.6 %all-gather.8.cloned.1.call-start = ((), (), s32[]{:S(2)}) async-start(), calls=%async_computation.2 | async-start | bytes 5242880 | tf_op jit(solution)/shard_map/all_gather | solution.py:120
  141.9 284.5 %all-gather.6.cloned.1.call-start = ((), (), s32[]{:S(2)}) async-start(), calls=%async_computation.1 | async-start | bytes 1310720 | tf_op jit(solution)/shard_map/all_gather | solution.py:120
  149.0 43.4 %collective-permute-start.6 = (f32[3600,128]{1,0:T(8,128)}, f32[3600,128]{1,0:T(8,128)}, u32[]{:S(2)}, u32[]{:S(2)}) collective-permute-start(f32[3600,128]{1,0:T(8,128)} %get-tuple-element.10.refs_0_), channel_id=1, source_target_pairs={{0,4},{1,5},{2,6},{3,7},{4,0},{5,1},{6,2},{7,3},{8,12},{9,13},{10,... | collective-permute-start | bytes 5529608 | tf_op jit(solution)/shard_map/ppermute | solution.py:114
  150.6 43.3 %collective-permute-start.3 = (f32[3600,128]{1,0:T(8,128)}, f32[3600,128]{1,0:T(8,128)S(1)}, u32[]{:S(2)}, u32[]{:S(2)}) collective-permute-start(f32[3600,128]{1,0:T(8,128)} %get-tuple-element.11.refs_1_), channel_id=1, source_target_pairs={{0,2},{1,3},{2,0},{3,1},{4,6},{5,7},{6,4},{7,5},{8,10},{9,11},{10,... | collective-permute-start | bytes 5529608 | tf_op jit(solution)/shard_map/ppermute | solution.py:114
  152.1 81.3 %collective-permute-start.2 = (f32[3600,128]{1,0:T(8,128)}, f32[3600,128]{1,0:T(8,128)S(1)}, u32[]{:S(2)}, u32[]{:S(2)}) collective-permute-start(f32[3600,128]{1,0:T(8,128)} %get-tuple-element.10.refs_0_), channel_id=1, source_target_pairs={{0,2},{1,3},{2,0},{3,1},{4,6},{5,7},{6,4},{7,5},{8,10},{9,11},{10,... | collective-permute-start | bytes 5529608 | tf_op jit(solution)/shard_map/ppermute | solution.py:114
  152.6 81.3 %collective-permute-start.7 = (f32[3600,128]{1,0:T(8,128)}, f32[3600,128]{1,0:T(8,128)}, u32[]{:S(2)}, u32[]{:S(2)}) collective-permute-start(f32[3600,128]{1,0:T(8,128)} %get-tuple-element.11.refs_1_), channel_id=1, source_target_pairs={{0,4},{1,5},{2,6},{3,7},{4,0},{5,1},{6,2},{7,3},{8,12},{9,13},{10,... | collective-permute-start | bytes 5529608 | tf_op jit(solution)/shard_map/ppermute | solution.py:114
  153.1 82.1 %collective-permute-start = (f32[3600,128]{1,0:T(8,128)}, f32[3600,128]{1,0:T(8,128)S(1)}, u32[]{:S(2)}, u32[]{:S(2)}) collective-permute-start(f32[3600,128]{1,0:T(8,128)} %get-tuple-element.10.refs_0_), channel_id=1, source_target_pairs={{0,1},{1,0},{2,3},{3,2},{4,5},{5,4},{6,7},{7,6},{8,9},{9,8},{10,11... | collective-permute-start | bytes 5529608 | tf_op jit(solution)/shard_map/ppermute | solution.py:114
  192.5 44.4 %collective-permute-start.1 = (f32[3600,128]{1,0:T(8,128)}, f32[3600,128]{1,0:T(8,128)S(1)}, u32[]{:S(2)}, u32[]{:S(2)}) collective-permute-start(f32[3600,128]{1,0:T(8,128)} %get-tuple-element.11.refs_1_), channel_id=1, source_target_pairs={{0,1},{1,0},{2,3},{3,2},{4,5},{5,4},{6,7},{7,6},{8,9},{9,8},{10,11... | collective-permute-start | bytes 5529608 | tf_op jit(solution)/shard_map/ppermute | solution.py:114
  193.9 76.8 %collective-permute-start.10 = (f32[3600,128]{1,0:T(8,128)}, f32[3600,128]{1,0:T(8,128)}, u32[]{:S(2)}, u32[]{:S(2)}) collective-permute-start(f32[3600,128]{1,0:T(8,128)} %collective-permute-done.6.refs_8_), channel_id=1, source_target_pairs={{0,2},{1,3},{2,0},{3,1},{4,6},{5,7},{6,4},{7,5},{8,10},{9,11},{10,... | collective-permute-start | bytes 5529608 | tf_op jit(solution)/shard_map/ppermute | solution.py:114
  233.4 37.8 %collective-permute-start.11 = (f32[3600,128]{1,0:T(8,128)S(1)}, f32[3600,128]{1,0:T(8,128)}, u32[]{:S(2)}, u32[]{:S(2)}) collective-permute-start(f32[3600,128]{1,0:T(8,128)S(1)} %collective-permute-done.3.refs_5_), channel_id=1, source_target_pairs={{0,4},{1,5},{2,6},{3,7},{4,0},{5,1},{6,2},{7,3},{8,12},{9,13},{10,... | collective-permute-start | bytes 5529608 | tf_op jit(solution)/shard_map/ppermute | solution.py:114
  233.9 37.3 %collective-permute-start.5 = (f32[3600,128]{1,0:T(8,128)S(1)}, f32[3600,128]{1,0:T(8,128)S(1)}, u32[]{:S(2)}, u32[]{:S(2)}) collective-permute-start(f32[3600,128]{1,0:T(8,128)S(1)} %collective-permute-done.3.refs_5_), channel_id=1, source_target_pairs={{0,1},{1,0},{2,3},{3,2},{4,5},{5,4},{6,7},{7,6},{8,9},{9,8},{10,11... | collective-permute-start | bytes 5529608 | tf_op jit(solution)/shard_map/ppermute | solution.py:114
  236.4 38.3 %collective-permute-start.8 = (f32[3600,128]{1,0:T(8,128)}, f32[3600,128]{1,0:T(8,128)}, u32[]{:S(2)}, u32[]{:S(2)}) collective-permute-start(f32[3600,128]{1,0:T(8,128)} %collective-permute-done.6.refs_8_), channel_id=1, source_target_pairs={{0,1},{1,0},{2,3},{3,2},{4,5},{5,4},{6,7},{7,6},{8,9},{9,8},{10,11... | collective-permute-start | bytes 5529608 | tf_op jit(solution)/shard_map/ppermute | solution.py:114
  238.2 36.5 %collective-permute-start.4 = (f32[3600,128]{1,0:T(8,128)S(1)}, f32[3600,128]{1,0:T(8,128)}, u32[]{:S(2)}, u32[]{:S(2)}) collective-permute-start(f32[3600,128]{1,0:T(8,128)S(1)} %collective-permute-done.2.refs_4_), channel_id=1, source_target_pairs={{0,1},{1,0},{2,3},{3,2},{4,5},{5,4},{6,7},{7,6},{8,9},{9,8},{10,11... | collective-permute-start | bytes 5529608 | tf_op jit(solution)/shard_map/ppermute | solution.py:114
  270.7 4.1 collective-permute-start.9
  271.2 6.3 %collective-permute-start.12 = (f32[3600,128]{1,0:T(8,128)}, f32[3600,128]{1,0:T(8,128)}, u32[]{:S(2)}, u32[]{:S(2)}) collective-permute-start(f32[3600,128]{1,0:T(8,128)} %collective-permute-done.10.refs_12_), channel_id=1, source_target_pairs={{0,1},{1,0},{2,3},{3,2},{4,5},{5,4},{6,7},{7,6},{8,9},{9,8},{10,11... | collective-permute-start | bytes 5529608 | tf_op jit(solution)/shard_map/ppermute | solution.py:114
  272.5 7.6 %collective-permute-start.13 = (f32[3600,128]{1,0:T(8,128)}, f32[3600,128]{1,0:T(8,128)}, u32[]{:S(2)}, u32[]{:S(2)}) collective-permute-start(f32[3600,128]{1,0:T(8,128)} %collective-permute-done.11.refs_13_), channel_id=1, source_target_pairs={{0,1},{1,0},{2,3},{3,2},{4,5},{5,4},{6,7},{7,6},{8,9},{9,8},{10,11... | collective-permute-start | bytes 5529608 | tf_op jit(solution)/shard_map/ppermute | solution.py:114
  289.2 21.4 %copy-start.1 = (f32[3600,128]{1,0:T(8,128)S(1)}, f32[3600,128]{1,0:T(8,128)}, u32[]{:S(2)}) copy-start(f32[3600,128]{1,0:T(8,128)} %get-tuple-element.10.refs_0_) | copy-start | bytes 5529604
  310.5 1.7 copy-start.3
  312.2 1.7 copy-start.9
  313.9 1.7 copy-start.15
  (29 other events, 42.3 us)
Sparse Core Ops, SparseCore 0:
  24.0 79.2 all-gather.13
  140.7 81.2 all-gather.11
  223.6 79.2 all-gather.9
  304.3 79.3 all-gather.7
  385.1 27.3 all-gather.5

commit v2 on v0

v2 whole, which is shorter than its diff:
```python
import functools

import jax
import jax.numpy as jnp
from jax import lax
from jax.experimental import pallas as pl
from jax.experimental.pallas import tpu as pltpu
from jax.sharding import PartitionSpec as P

ROWS = 720
WIDE = 512
VMEM_BYTES = 60 * 2**20


def params():
    return pltpu.CompilerParams(vmem_limit_bytes=VMEM_BYTES)


def moved(bytes_accessed, flops=0):
    return pl.CostEstimate(
        flops=flops, bytes_accessed=bytes_accessed, transcendentals=0
    )


def chunks_of(columns, line):
    if columns == 1920 and line == 4:
        return [
            (1024, 256, 256, False),
            (0, 512, 512, False),
            (512, 512, 512, False),
            (1536, 384, 384, True),
            (1280, 256, 256, False),
        ]
    wide = [(n, WIDE, WIDE, False) for n in range(0, columns - WIDE + 1, WIDE)]
    start = len(wide) * WIDE
    return wide + ([(start, columns - start, WIDE, False)] if start < columns else [])


def holder(here, n):
    away = here ^ n
    if away < 2:
        return away
    if here in (0, 3):
        return 3 if away == 2 else 5
    return 4 if away == 2 else 2


def along_line(own):
    inner, outer = [(1, 2), (2, 1)], [(1, 0), (2, 3)]
    send = lambda x, pairs: lax.ppermute(x, "ga", pairs)
    first = send(own, outer + [(0, 1), (3, 2)])
    second = send(own, inner)
    fourth = send(first, inner)
    third = send(second, outer)
    fifth = send(fourth, outer)
    return [own, first, second, third, fourth, fifth]


def cut_kernel(t_ref, out_ref):
    groups, _, rows = out_ref.shape
    for n in range(groups):
        out_ref[n] = t_ref[:, n * rows : (n + 1) * rows]


def cut(columns, groups, half):
    depth, pairs = columns.shape
    shape = (groups, depth // 2, pairs // groups)
    return pl.pallas_call(
        cut_kernel,
        grid=(1,),
        in_specs=[pl.BlockSpec((depth // 2, pairs), lambda i: (half, 0))],
        out_specs=pl.BlockSpec(shape, lambda i: (0, 0, 0)),
        out_shape=jax.ShapeDtypeStruct(shape, jnp.float32),
        compiler_params=params(),
        cost_estimate=moved(4 * depth * pairs),
    )(columns)


def turn_kernel(t_ref, out_ref):
    out_ref[...] = t_ref[...].T


def turn(columns):
    depth, rows = columns.shape
    width = 1024
    return pl.pallas_call(
        turn_kernel,
        grid=(pl.cdiv(rows, width),),
        in_specs=[pl.BlockSpec((depth, width), lambda i: (0, i))],
        out_specs=pl.BlockSpec((width, depth), lambda i: (i, 0)),
        out_shape=jax.ShapeDtypeStruct((rows, depth), jnp.float32),
        compiler_params=params(),
        cost_estimate=moved(8 * depth * rows),
    )(columns)


def split(x):
    high = x.astype(jnp.bfloat16)
    return high, (x - high.astype(jnp.float32)).astype(jnp.bfloat16)


def halve_kernel(blocks, *refs):
    high_ref, low_ref = refs[-2:]
    width = refs[0].shape[1]
    for n in range(blocks):
        high, low = split(refs[n][...])
        high_ref[:, n * width : (n + 1) * width] = high
        low_ref[:, n * width : (n + 1) * width] = low


def halve(parts, held, group, depth):
    blocks = len(parts)
    rows, width = parts[0].shape
    whole = jax.ShapeDtypeStruct((rows, depth), jnp.bfloat16)
    in_specs = [pl.BlockSpec((ROWS, width), lambda i: (i, 0))] * blocks
    in_specs += [pl.BlockSpec(memory_space=pl.ANY)] * len(held)
    out_spec = pl.BlockSpec((ROWS, width * blocks), lambda i: (i, group))
    return pl.pallas_call(
        functools.partial(halve_kernel, blocks),
        grid=(pl.cdiv(rows, ROWS),),
        in_specs=in_specs,
        out_specs=[out_spec, out_spec],
        out_shape=[whole, whole],
        input_output_aliases={blocks + n: n for n in range(len(held))},
        compiler_params=params(),
        cost_estimate=moved(8 * rows * width * blocks),
    )(*parts, *held)


def product_kernel(line, devices, gathered, place_ref, t_high, t_low, *refs):
    out_ref, w, w_high, w_low, arrived = refs[-5:]
    depth, width = w.shape
    size = depth // line

    @pl.when(pl.program_id(0) == 0)
    def _():
        if gathered:
            whole = pltpu.make_async_copy(refs[0], w, arrived.at[0])
            whole.start()
            whole.wait()
        else:

            def copy(source, n):
                return pltpu.make_async_copy(
                    refs[source], w.at[pl.ds(n * size, size)], arrived.at[n]
                )

            for here in range(line):

                @pl.when(place_ref[1] == here)
                def _():
                    for n in range(line):
                        copy(holder(here, n), n).start()

            for n in range(line):
                copy(0, n).wait()
        block = depth // devices
        piece = block // line // 2
        for n in range(devices):
            start = (place_ref[0] ^ n) * block
            for half in range(2):
                rows = [
                    w[pl.ds(pl.multiple_of(start, block) + (2 * m + half) * piece, piece), :]
                    for m in range(line)
                ]
                high, low = split(jnp.concatenate(rows, axis=0))
                to = pl.ds((2 * n + half) * (block // 2), block // 2)
                w_high[to, :] = high
                w_low[to, :] = low

    dot = functools.partial(jnp.dot, preferred_element_type=jnp.float32)
    total = dot(t_low[...], w_high[...])
    total += dot(t_high[...], w_low[...])
    total += dot(t_high[...], w_high[...])
    out_ref[:, :width] = 0.5 * total


def product(line, devices, place, t_high, t_low, shards, out, chunk, full):
    start, width, block, by_line = chunk
    rows, depth = t_high.shape
    t_spec = pl.BlockSpec((ROWS, depth), lambda i, p: (i, 0))
    anywhere = pl.BlockSpec(memory_space=pl.ANY)
    operands = [place, t_high, t_low, *shards]
    aliases = {}
    if out is not None:
        aliases = {len(operands): 0}
        operands.append(out)
    return pl.pallas_call(
        functools.partial(product_kernel, line, devices, not by_line),
        grid_spec=pltpu.PrefetchScalarGridSpec(
            num_scalar_prefetch=1,
            grid=(pl.cdiv(rows, ROWS),),
            in_specs=[t_spec, t_spec] + [anywhere] * (len(operands) - 3),
            out_specs=pl.BlockSpec((ROWS, block), lambda i, p: (i, start // block)),
            scratch_shapes=[
                pltpu.VMEM((depth, width), jnp.float32),
                pltpu.VMEM((depth, width), jnp.bfloat16),
                pltpu.VMEM((depth, width), jnp.bfloat16),
                pltpu.SemaphoreType.DMA((line,)),
            ],
        ),
        out_shape=jax.ShapeDtypeStruct((rows, full), jnp.float32),
        input_output_aliases=aliases,
        compiler_params=params(),
        cost_estimate=moved(
            4 * (rows * depth + depth * width + rows * width),
            6 * rows * depth * width,
        ),
    )(*operands)


def after(value, *others):
    return lax.optimization_barrier((value, *others))[0]


def per_device(line, devices, amplitudes, integrals):
    columns = integrals.shape[1]
    depth = integrals.shape[0] * line

    chunks = chunks_of(columns, line)

    def piece(chunk, source):
        return lax.slice_in_dim(source, chunk[0], chunk[0] + chunk[1], axis=1)

    def gather(x):
        return [lax.all_gather(x, "ga", axis=0, tiled=True)]

    first, amplitudes = lax.optimization_barrier((piece(chunks[0], integrals), amplitudes))
    shards = {chunks[0]: gather(first)}
    for chunk in chunks[1:]:
        if not chunk[3]:
            shards[chunk] = gather(piece(chunk, integrals))

    regrouped = []
    for half in range(2):
        blocks = cut(amplitudes.T, line, half)
        blocks = lax.all_to_all(blocks, "ga", split_axis=0, concat_axis=0, tiled=True)
        regrouped.append(blocks.reshape(-1, blocks.shape[-1]))
    regrouped[1] = after(regrouped[1], *shards[chunks[0]])

    def swap(x, mask):
        return lax.ppermute(x, "ka", [(d, d ^ mask) for d in range(devices)])

    masks = [1 << bit for bit in range(1, devices.bit_length() - 1)]
    halves = []
    for half, order in zip(regrouped, (masks[::-1], masks)):
        held = {0: turn(half)}
        for mask in (*order, 1):
            held |= {n ^ mask: swap(block, mask) for n, block in held.items()}
        halves.append(held)

    rest = after(integrals, halves[0][devices - 2], halves[1][devices - 2])
    shards |= {chunk: along_line(piece(chunk, rest)) for chunk in chunks if chunk[3]}

    whole = ()
    for group in range(devices // 2):
        parts = [held[n] for n in (2 * group, 2 * group + 1) for held in halves]
        whole = halve(parts, whole, group, depth)

    place = jnp.stack([lax.axis_index("ka"), lax.axis_index("ga")])
    moving = [shards[chunk] for chunk in chunks if chunk[3]]
    out = None
    for n, chunk in enumerate(chunks):
        if moving and n in (1, 2):
            out = after(out, *moving[0][2 * n - 1 : 2 * n + 1])
        out = product(line, devices, place, *whole, shards[chunk], out, chunk, columns)
    return out


def solution(mesh):
    placed = (P(None, ("ka", "ga")), P("ga", "ka"))
    return jax.shard_map(
        functools.partial(per_device, mesh.shape["ga"], mesh.shape["ka"]),
        mesh=mesh,
        in_specs=placed,
        out_specs=P("ga", "ka"),
        check_vma=False,
    )
```

time: 720 us -> 509 us (0.71)
  matrix products: 205 us -> 0 us
  blocking collectives: 190 us -> 0 us
  Pallas kernels: 0 us -> 183 us
  waiting for transfers between devices: 302 us -> 268 us
  starting transfers between devices: 0.04 us -> 31.7 us
    all_gather x2 -> x4, waiting for transfers between devices: 301 us -> 0.07 us  [gather(): return [lax.all_gather(x, 'ga', axis=0, tiled=True)]]
    dot_general x1 -> x0, matrix products: 205 us -> none  [per_device(): jnp.dot(full_rows, lax.all_gather(integrals, 'ga', axis=0, tiled=True), p...]
    all_to_all x1 -> x0, blocking collectives: 190 us -> none  [per_device(): lax.all_to_all(amplitudes, 'ga', split_axis=0, concat_axis=1, tiled=True)]
    pallas_call x0 -> x13, Pallas kernels: none -> 183 us  [the longest x5 136 us: product(): pl.pallas_call(functools.partial(product_kernel, line, devices, not by_li...]
    all_to_all x0 -> x2, waiting for transfers between devices: none -> 154 us  [per_device(): lax.all_to_all(blocks, 'ga', split_axis=0, concat_axis=0, tiled=True)]
    ppermute x0 -> x19, waiting for transfers between devices: none -> 113 us  [the longest x14 78.1 us: swap(): return lax.ppermute(x, 'ka', [(d, d ^ mask) for d in range(devices)])]
    ppermute x0 -> x19, starting transfers between devices: none -> 19.6 us  [the longest x5 10.9 us: along_line(): send = lambda x, pairs: lax.ppermute(x, 'ga', pairs)]
    all_to_all x0 -> x2, starting transfers between devices: none -> 12.1 us  [per_device(): lax.all_to_all(blocks, 'ga', split_axis=0, concat_axis=0, tiled=True)]
  transfers between devices with their start and end apart: 2 -> 25, of which waited for: 2 -> 7; matrix products, arithmetic and copies ran while one was open for 0% -> 1% of each run, Pallas kernels for 0% -> 32%
where the time goes in v2:
time: 509 us; the launch traced here: 507 us
  waiting for transfers between devices  268 us (53%)
  Pallas kernels  183 us (36%)
  starting transfers between devices  31.7 us (6%)
  between operations  13.4 us (3%)
  local copies, waits for them, and re-layouts  10 us (2%)
    all_to_all x2, waiting for transfers between devices, per_device(): lax.all_to_all(blocks, 'ga', split_axis=0, concat_axis=0, tiled=True)  154 us
    pallas_call x5, Pallas kernels, product(): pl.pallas_call(functools.partial(product_kernel, line, devices, not by_li...  136 us
    ppermute x14, waiting for transfers between devices, swap(): return lax.ppermute(x, 'ka', [(d, d ^ mask) for d in range(devices)])  78.1 us
    ppermute x5, waiting for transfers between devices, along_line(): send = lambda x, pairs: lax.ppermute(x, 'ga', pairs)  35 us
    pallas_call x4, Pallas kernels, halve(): pl.pallas_call(functools.partial(halve_kernel, blocks), grid=(pl.cdiv(row...  32.9 us
    all_to_all x2, starting transfers between devices, per_device(): lax.all_to_all(blocks, 'ga', split_axis=0, concat_axis=0, tiled=True)  12.1 us
    ppermute x5, starting transfers between devices, along_line(): send = lambda x, pairs: lax.ppermute(x, 'ga', pairs)  10.9 us
  transfers between devices with their start and end apart: 25, of which 7 were waited for; matrix products, arithmetic and copies ran while one was open for 1% of the time, Pallas kernels for 32%

profile of v2, /device:TPU:16, one launch (start us, length us, event | category | flops | bytes accessed | tf_op | source)
XLA Modules:
  0.0 507.4 jit_solution(5738477519953677753)
XLA Ops:
  8.9 3.1 fusion
  12.1 3.2 shard_map.28
  15.2 5.2 %all-to-all-start = ((f32[4,32,3600]{2,1,0:T(8,128)}), f32[4,32,3600]{2,1,0:T(8,128)S(1)}, u32[]{:S(2)}, u32[]{:S(2)}) async-start(f32[4,32,3600]{2,1,0:T(8,128)} %shard_map.28), calls=%async_computation | async-start | bytes 3801088 | tf_op jit(solution)/shard_map/all_to_all | solution.py:237
  20.5 3.2 shard_map.30
  23.7 69.7 %all-to-all-done = f32[4,32,3600]{2,1,0:T(8,128)S(1)} async-done(((f32[4,32,3600]{2,1,0:T(8,128)}), f32[4,32,3600]{2,1,0:T(8,128)S(1)}, u32[]{:S(2)}, u32[]{:S(2)}) %all-to-all-start) | async-done | bytes 1843232 | tf_op jit(solution)/shard_map/all_to_all | solution.py:237
  94.7 6.9 %all-to-all-start.1 = ((f32[4,32,3600]{2,1,0:T(8,128)}), f32[4,32,3600]{2,1,0:T(8,128)S(1)}, u32[]{:S(2)}, u32[]{:S(2)}) async-start(f32[4,32,3600]{2,1,0:T(8,128)} %shard_map.30), calls=%async_computation.1 | async-start | bytes 3801088 | tf_op jit(solution)/shard_map/all_to_all | solution.py:237
  102.3 4.0 shard_map.29.refs_0_
  109.3 84.6 %all-to-all-done.1 = f32[4,32,3600]{2,1,0:T(8,128)S(1)} async-done(((f32[4,32,3600]{2,1,0:T(8,128)}), f32[4,32,3600]{2,1,0:T(8,128)S(1)}, u32[]{:S(2)}, u32[]{:S(2)}) %all-to-all-start.1) | async-done | bytes 1843232 | tf_op jit(solution)/shard_map/all_to_all | solution.py:237
  195.1 3.9 shard_map.31.refs_1_
  202.8 39.6 %collective-permute-done.2.refs_1_ = f32[3600,128]{1,0:T(8,128)S(1)} collective-permute-done((f32[3600,128]{1,0:T(8,128)}, f32[3600,128]{1,0:T(8,128)S(1)}, u32[]{:S(2)}, u32[]{:S(2)}) %collective-permute-start.2) | collective-permute-done | bytes 1843232 | tf_op jit(solution)/shard_map/ppermute | solution.py:242
  244.5 32.5 %collective-permute-done.1.refs_0_ = f32[3600,128]{1,0:T(8,128)} collective-permute-done((f32[3600,128]{1,0:T(8,128)}, f32[3600,128]{1,0:T(8,128)}, u32[]{:S(2)}, u32[]{:S(2)}) %collective-permute-start.1) | collective-permute-done | bytes 1843232 | tf_op jit(solution)/shard_map/ppermute | solution.py:242
  276.9 6.0 %collective-permute-done.3.refs_1_ = f32[3600,128]{1,0:T(8,128)} collective-permute-done((f32[3600,128]{1,0:T(8,128)S(1)}, f32[3600,128]{1,0:T(8,128)}, u32[]{:S(2)}, u32[]{:S(2)}) %collective-permute-start.3) | collective-permute-done | bytes 1843232 | tf_op jit(solution)/shard_map/ppermute | solution.py:242
  286.5 3.5 collective-permute-start.15
  290.0 19.4 %collective-permute-done.14.refs_1_ = f32[512,384]{1,0:T(8,128)S(1)} collective-permute-done((f32[512,384]{1,0:T(8,128)S(1)}, f32[512,384]{1,0:T(8,128)S(1)}, u32[]{:S(2)}, u32[]{:S(2)}) %collective-permute-start.14) | collective-permute-done | bytes 786464 | tf_op jit(solution)/shard_map/ppermute | solution.py:50
  312.0 8.2 %shard_map.32 = (bf16[3600,2048]{1,0:T(8,128)(2,1)}, bf16[3600,2048]{1,0:T(8,128)(2,1)}) custom-call(f32[3600,128]{1,0:T(8,128)} %shard_map.29.refs_0_, f32[3600,128]{1,0:T(8,128)} %shard_map.31.refs_1_, f32[3600,128]{1,0:T(8,128)} %collective-permute-done.12.refs_2_, f32[3600,128]{1,0:T(8,128)} %copy-done.3), custom_call_target="tpu_custom_call" | custom-call | bytes 14745600 | tf_op jit(solution)/shard_map/pallas_call | solution.py:118
  320.2 8.3 %shard_map.33 = (bf16[3600,2048]{1,0:T(8,128)(2,1)}, bf16[3600,2048]{1,0:T(8,128)(2,1)}) custom-call(f32[3600,128]{1,0:T(8,128)} %collective-permute-done.9.refs_0_, f32[3600,128]{1,0:T(8,128)} %copy-done.4, f32[3600,128]{1,0:T(8,128)} %copy-done.5, f32[3600,128]{1,0:T(8,128)} %copy-done.7, ...), custom_call_target="tpu_custom_call", output_to_operand_aliasing={{0}: (4, {}), {1}: (5, {})} | custom-call | bytes 14745600 | tf_op jit(solution)/shard_map/pallas_call | solution.py:118
  328.5 8.2 %shard_map.34 = (bf16[3600,2048]{1,0:T(8,128)(2,1)}, bf16[3600,2048]{1,0:T(8,128)(2,1)}) custom-call(f32[3600,128]{1,0:T(8,128)} %collective-permute-done.refs_0_, f32[3600,128]{1,0:T(8,128)} %collective-permute-done.6.refs_1_, f32[3600,128]{1,0:T(8,128)} %copy-done.6, ...), custom_call_target="tpu_custom_call", output_to_operand_aliasing={{0}: (4, {}), {1}: (5, {})} | custom-call | bytes 14745600 | tf_op jit(solution)/shard_map/pallas_call | solution.py:118
  338.4 15.6 %collective-permute-done.17.refs_4_ = f32[512,384]{1,0:T(8,128)} collective-permute-done((f32[512,384]{1,0:T(8,128)S(1)}, f32[512,384]{1,0:T(8,128)}, u32[]{:S(2)}, u32[]{:S(2)}) %collective-permute-start.17) | collective-permute-done | bytes 786464 | tf_op jit(solution)/shard_map/ppermute | solution.py:50
  355.6 8.2 %shard_map.35 = (bf16[3600,2048]{1,0:T(8,128)(2,1)}, bf16[3600,2048]{1,0:T(8,128)(2,1)}) custom-call(f32[3600,128]{1,0:T(8,128)} %collective-permute-done.1.refs_0_, f32[3600,128]{1,0:T(8,128)} %collective-permute-done.3.refs_1_, f32[3600,128]{1,0:T(8,128)} %collective-permute-done.4.refs_2_, ...), custom_call_target="tpu_custom_call", output_to_operand_aliasing={{0}: (4, {}), {1}: (5, {})} | custom-call | bytes 14745600 | tf_op jit(solution)/shard_map/pallas_call | solution.py:118
  363.7 20.4 %shard_map.36.refs_1_ = f32[3600,1920]{1,0:T(8,128)} custom-call(s32[2]{0:T(128)} %pad_add_fusion.place_ref, bf16[3600,2048]{1,0:T(8,128)(2,1)} %get-tuple-element.28.t_high, bf16[3600,2048]{1,0:T(8,128)(2,1)} %get-tuple-element.29.t_low, f32[2048,256]{1,0:T(8,128)} %all-gather.5.cloned.1.call-done.refs_0_), custom_call_target="tpu_custom_call" | custom-call | flops 11324620800 | bytes 35274752 | tf_op jit(solution)/shard_map/pallas_call | solution.py:188
  384.2 32.0 %shard_map.37.refs_1_ = f32[3600,1920]{1,0:T(8,128)} custom-call(s32[2]{0:T(128)} %pad_add_fusion.place_ref, bf16[3600,2048]{1,0:T(8,128)(2,1)} %get-tuple-element.28.t_high, bf16[3600,2048]{1,0:T(8,128)(2,1)} %get-tuple-element.29.t_low, f32[2048,512]{1,0:T(8,128)} %all-gather.11.cloned.1.call-done.refs_0_, ...), custom_call_target="tpu_custom_call", output_to_operand_aliasing={{}: (4, {})} | custom-call | flops 22649241600 | bytes 41058304 | tf_op jit(solution)/shard_map/pallas_call | solution.py:188
  416.2 32.0 %shard_map.38.refs_6_ = f32[3600,1920]{1,0:T(8,128)} custom-call(s32[2]{0:T(128)} %pad_add_fusion.place_ref, bf16[3600,2048]{1,0:T(8,128)(2,1)} %get-tuple-element.28.t_high, bf16[3600,2048]{1,0:T(8,128)(2,1)} %get-tuple-element.29.t_low, f32[2048,512]{1,0:T(8,128)} %all-gather.9.cloned.1.call-done.refs_0_, ...), custom_call_target="tpu_custom_call", output_to_operand_aliasing={{}: (4, {})} | custom-call | flops 22649241600 | bytes 41058304 | tf_op jit(solution)/shard_map/pallas_call | solution.py:188
  449.1 31.3 %shard_map.39.refs_1_ = f32[3600,1920]{1,0:T(8,128)} custom-call(s32[2]{0:T(128)} %pad_add_fusion.place_ref, bf16[3600,2048]{1,0:T(8,128)(2,1)} %get-tuple-element.28.t_high, bf16[3600,2048]{1,0:T(8,128)(2,1)} %get-tuple-element.29.t_low, f32[512,384]{1,0:T(8,128)} %copy-done.2, f32[512,384]{1,0:T(8,128)} %copy-done.8, ...), custom_call_target="tpu_custom_call", output_to_operand_aliasing={{}: (9, {})} | custom-call | flops 16986931200 | bytes 38166528 | tf_op jit(solution)/shard_map/pallas_call | solution.py:188
  480.5 20.4 %shard_map.40 = f32[3600,1920]{1,0:T(8,128)} custom-call(s32[2]{0:T(128)} %pad_add_fusion.place_ref, bf16[3600,2048]{1,0:T(8,128)(2,1)} %get-tuple-element.28.t_high, bf16[3600,2048]{1,0:T(8,128)(2,1)} %get-tuple-element.29.t_low, f32[2048,256]{1,0:T(8,128)} %all-gather.7.cloned.1.call-done.refs_0_, ...), custom_call_target="tpu_custom_call", output_to_operand_aliasing={{}: (4, {})} | custom-call | flops 11324620800 | bytes 35274752 | tf_op jit(solution)/shard_map/pallas_call | solution.py:188
  (69 shorter events, 24.5 us)
Async XLA Ops:
  6.5 187.4 %all-gather.5.cloned.1.call-start = ((), (), s32[]{:S(2)}) async-start(), calls=%async_computation.2 | async-start | bytes 2621440 | tf_op jit(solution)/shard_map/all_gather | solution.py:226
  8.9 375.3 %all-gather.11.cloned.1.call-start = ((), (), s32[]{:S(2)}) async-start(), calls=%async_computation.5 | async-start | bytes 5242880 | tf_op jit(solution)/shard_map/all_gather | solution.py:226
  15.2 78.2 %all-to-all-start = ((f32[4,32,3600]{2,1,0:T(8,128)}), f32[4,32,3600]{2,1,0:T(8,128)S(1)}, u32[]{:S(2)}, u32[]{:S(2)}) async-start(f32[4,32,3600]{2,1,0:T(8,128)} %shard_map.28), calls=%async_computation | async-start | bytes 3801088 | tf_op jit(solution)/shard_map/all_to_all | solution.py:237
  94.7 99.2 %all-to-all-start.1 = ((f32[4,32,3600]{2,1,0:T(8,128)}), f32[4,32,3600]{2,1,0:T(8,128)S(1)}, u32[]{:S(2)}, u32[]{:S(2)}) async-start(f32[4,32,3600]{2,1,0:T(8,128)} %shard_map.30), calls=%async_computation.1 | async-start | bytes 3801088 | tf_op jit(solution)/shard_map/all_to_all | solution.py:237
  101.5 314.7 %all-gather.9.cloned.1.call-start = ((), (), s32[]{:S(2)}) async-start(), calls=%async_computation.4 | async-start | bytes 5242880 | tf_op jit(solution)/shard_map/all_gather | solution.py:226
  102.3 378.2 %all-gather.7.cloned.1.call-start = ((), (), s32[]{:S(2)}) async-start(), calls=%async_computation.3 | async-start | bytes 2621440 | tf_op jit(solution)/shard_map/all_gather | solution.py:226
  106.3 94.2 %collective-permute-start.12 = (f32[3600,128]{1,0:T(8,128)}, f32[3600,128]{1,0:T(8,128)}, u32[]{:S(2)}, u32[]{:S(2)}) collective-permute-start(f32[3600,128]{1,0:T(8,128)} %shard_map.29.refs_0_), channel_id=1, source_target_pairs={{0,1},{1,0},{2,3},{3,2},{4,5},{5,4},{6,7},{7,6},{8,9},{9,8},{10,11... | collective-permute-start | bytes 5529608 | tf_op jit(solution)/shard_map/ppermute | solution.py:242
  106.3 95.7 %collective-permute-start.9 = (f32[3600,128]{1,0:T(8,128)}, f32[3600,128]{1,0:T(8,128)}, u32[]{:S(2)}, u32[]{:S(2)}) collective-permute-start(f32[3600,128]{1,0:T(8,128)} %shard_map.29.refs_0_), channel_id=1, source_target_pairs={{0,2},{1,3},{2,0},{3,1},{4,6},{5,7},{6,4},{7,5},{8,10},{9,11},{10,... | collective-permute-start | bytes 5529608 | tf_op jit(solution)/shard_map/ppermute | solution.py:242
  107.8 94.5 %collective-permute-start = (f32[3600,128]{1,0:T(8,128)}, f32[3600,128]{1,0:T(8,128)}, u32[]{:S(2)}, u32[]{:S(2)}) collective-permute-start(f32[3600,128]{1,0:T(8,128)} %shard_map.29.refs_0_), channel_id=1, source_target_pairs={{0,4},{1,5},{2,6},{3,7},{4,0},{5,1},{6,2},{7,3},{8,12},{9,13},{10,... | collective-permute-start | bytes 5529608 | tf_op jit(solution)/shard_map/ppermute | solution.py:242
  199.1 43.3 %collective-permute-start.2 = (f32[3600,128]{1,0:T(8,128)}, f32[3600,128]{1,0:T(8,128)S(1)}, u32[]{:S(2)}, u32[]{:S(2)}) collective-permute-start(f32[3600,128]{1,0:T(8,128)} %shard_map.31.refs_1_), channel_id=1, source_target_pairs={{0,2},{1,3},{2,0},{3,1},{4,6},{5,7},{6,4},{7,5},{8,10},{9,11},{10,... | collective-permute-start | bytes 5529608 | tf_op jit(solution)/shard_map/ppermute | solution.py:242
  200.5 43.3 %collective-permute-start.13 = (f32[3600,128]{1,0:T(8,128)}, f32[3600,128]{1,0:T(8,128)S(1)}, u32[]{:S(2)}, u32[]{:S(2)}) collective-permute-start(f32[3600,128]{1,0:T(8,128)} %shard_map.31.refs_1_), channel_id=1, source_target_pairs={{0,1},{1,0},{2,3},{3,2},{4,5},{5,4},{6,7},{7,6},{8,9},{9,8},{10,11... | collective-permute-start | bytes 5529608 | tf_op jit(solution)/shard_map/ppermute | solution.py:242
  200.5 43.3 %collective-permute-start.6 = (f32[3600,128]{1,0:T(8,128)}, f32[3600,128]{1,0:T(8,128)}, u32[]{:S(2)}, u32[]{:S(2)}) collective-permute-start(f32[3600,128]{1,0:T(8,128)} %shard_map.31.refs_1_), channel_id=1, source_target_pairs={{0,4},{1,5},{2,6},{3,7},{4,0},{5,1},{6,2},{7,3},{8,12},{9,13},{10,... | collective-permute-start | bytes 5529608 | tf_op jit(solution)/shard_map/ppermute | solution.py:242
  202.0 42.4 %collective-permute-start.10 = (f32[3600,128]{1,0:T(8,128)}, f32[3600,128]{1,0:T(8,128)S(1)}, u32[]{:S(2)}, u32[]{:S(2)}) collective-permute-start(f32[3600,128]{1,0:T(8,128)} %collective-permute-done.9.refs_0_), channel_id=1, source_target_pairs={{0,1},{1,0},{2,3},{3,2},{4,5},{5,4},{6,7},{7,6},{8,9},{9,8},{10,11... | collective-permute-start | bytes 5529608 | tf_op jit(solution)/shard_map/ppermute | solution.py:242
  202.2 74.7 %collective-permute-start.1 = (f32[3600,128]{1,0:T(8,128)}, f32[3600,128]{1,0:T(8,128)}, u32[]{:S(2)}, u32[]{:S(2)}) collective-permute-start(f32[3600,128]{1,0:T(8,128)} %collective-permute-done.refs_0_), channel_id=1, source_target_pairs={{0,2},{1,3},{2,0},{3,1},{4,6},{5,7},{6,4},{7,5},{8,10},{9,11},{10,... | collective-permute-start | bytes 5529608 | tf_op jit(solution)/shard_map/ppermute | solution.py:242
  242.4 40.5 %collective-permute-start.3 = (f32[3600,128]{1,0:T(8,128)S(1)}, f32[3600,128]{1,0:T(8,128)}, u32[]{:S(2)}, u32[]{:S(2)}) collective-permute-start(f32[3600,128]{1,0:T(8,128)S(1)} %collective-permute-done.2.refs_1_), channel_id=1, source_target_pairs={{0,4},{1,5},{2,6},{3,7},{4,0},{5,1},{6,2},{7,3},{8,12},{9,13},{10,... | collective-permute-start | bytes 5529608 | tf_op jit(solution)/shard_map/ppermute | solution.py:242
  243.9 40.3 %collective-permute-start.7 = (f32[3600,128]{1,0:T(8,128)}, f32[3600,128]{1,0:T(8,128)S(1)}, u32[]{:S(2)}, u32[]{:S(2)}) collective-permute-start(f32[3600,128]{1,0:T(8,128)} %collective-permute-done.refs_0_), channel_id=1, source_target_pairs={{0,1},{1,0},{2,3},{3,2},{4,5},{5,4},{6,7},{7,6},{8,9},{9,8},{10,11... | collective-permute-start | bytes 5529608 | tf_op jit(solution)/shard_map/ppermute | solution.py:242
  243.9 42.6 %collective-permute-start.11 = (f32[3600,128]{1,0:T(8,128)S(1)}, f32[3600,128]{1,0:T(8,128)S(1)}, u32[]{:S(2)}, u32[]{:S(2)}) collective-permute-start(f32[3600,128]{1,0:T(8,128)S(1)} %collective-permute-done.2.refs_1_), channel_id=1, source_target_pairs={{0,1},{1,0},{2,3},{3,2},{4,5},{5,4},{6,7},{7,6},{8,9},{9,8},{10,11... | collective-permute-start | bytes 5529608 | tf_op jit(solution)/shard_map/ppermute | solution.py:242
  244.4 84.2 %collective-permute-start.8 = (f32[3600,128]{1,0:T(8,128)}, f32[3600,128]{1,0:T(8,128)}, u32[]{:S(2)}, u32[]{:S(2)}) collective-permute-start(f32[3600,128]{1,0:T(8,128)} %collective-permute-done.6.refs_1_), channel_id=1, source_target_pairs={{0,1},{1,0},{2,3},{3,2},{4,5},{5,4},{6,7},{7,6},{8,9},{9,8},{10,11... | collective-permute-start | bytes 5529608 | tf_op jit(solution)/shard_map/ppermute | solution.py:242
  276.9 78.6 %collective-permute-start.4 = (f32[3600,128]{1,0:T(8,128)}, f32[3600,128]{1,0:T(8,128)}, u32[]{:S(2)}, u32[]{:S(2)}) collective-permute-start(f32[3600,128]{1,0:T(8,128)} %collective-permute-done.1.refs_0_), channel_id=1, source_target_pairs={{0,1},{1,0},{2,3},{3,2},{4,5},{5,4},{6,7},{7,6},{8,9},{9,8},{10,11... | collective-permute-start | bytes 5529608 | tf_op jit(solution)/shard_map/ppermute | solution.py:242
  283.0 72.6 %collective-permute-start.5 = (f32[3600,128]{1,0:T(8,128)}, f32[3600,128]{1,0:T(8,128)}, u32[]{:S(2)}, u32[]{:S(2)}) collective-permute-start(f32[3600,128]{1,0:T(8,128)} %collective-permute-done.3.refs_1_), channel_id=1, source_target_pairs={{0,1},{1,0},{2,3},{3,2},{4,5},{5,4},{6,7},{7,6},{8,9},{9,8},{10,11... | collective-permute-start | bytes 5529608 | tf_op jit(solution)/shard_map/ppermute | solution.py:242
  286.5 50.3 %collective-permute-start.15 = (f32[512,384]{1,0:T(8,128)S(1)}, f32[512,384]{1,0:T(8,128)}, u32[]{:S(2)}, u32[]{:S(2)}) collective-permute-start(f32[512,384]{1,0:T(8,128)S(1)} %slice.17.refs_0_), channel_id=1, source_target_pairs={{8,16},{16,8},{9,17},{17,9},{10,18},{18,10},{11,19},{19,11},{12,20... | collective-permute-start | bytes 2359304 | tf_op jit(solution)/shard_map/ppermute | solution.py:50
  309.4 44.7 %collective-permute-start.17 = (f32[512,384]{1,0:T(8,128)S(1)}, f32[512,384]{1,0:T(8,128)}, u32[]{:S(2)}, u32[]{:S(2)}) collective-permute-start(f32[512,384]{1,0:T(8,128)S(1)} %collective-permute-done.14.refs_1_), channel_id=1, source_target_pairs={{8,16},{16,8},{9,17},{17,9},{10,18},{18,10},{11,19},{19,11},{12,20... | collective-permute-start | bytes 2359304 | tf_op jit(solution)/shard_map/ppermute | solution.py:50
  336.8 79.4 %collective-permute-start.16 = (f32[512,384]{1,0:T(8,128)}, f32[512,384]{1,0:T(8,128)S(1)}, u32[]{:S(2)}, u32[]{:S(2)}) collective-permute-start(f32[512,384]{1,0:T(8,128)} %collective-permute-done.15.refs_2_), channel_id=1, source_target_pairs={{8,0},{16,24},{9,1},{17,25},{10,2},{18,26},{11,3},{19,27},{12,4},{... | collective-permute-start | bytes 2359304 | tf_op jit(solution)/shard_map/ppermute | solution.py:50
  354.0 94.2 %collective-permute-start.18 = (f32[512,384]{1,0:T(8,128)}, f32[512,384]{1,0:T(8,128)S(1)}, u32[]{:S(2)}, u32[]{:S(2)}) collective-permute-start(f32[512,384]{1,0:T(8,128)} %collective-permute-done.17.refs_4_), channel_id=1, source_target_pairs={{8,0},{16,24},{9,1},{17,25},{10,2},{18,26},{11,3},{19,27},{12,4},{... | collective-permute-start | bytes 2359304 | tf_op jit(solution)/shard_map/ppermute | solution.py:50
  (12 other events, 333.1 us)
Sparse Core Ops, SparseCore 0:
  9.0 80.3 all-gather.4
  90.9 119.0 all-gather.10
  211.6 86.1 all-gather.8
  311.5 50.9 all-gather.6
